TPU v7x, 32 devices: a whole 2x2x4 slice. The times are simulated.
32 devices in a mesh: groups: 2 (over y), samp: 4 (over x, core), par: 4 (over z).
Axes of the slice: x: 2, y: 2, z: 4, core: 2. Of those that a mesh axis runs over, the one named last changes fastest.
Arguments:
- log_derivs: float32 [2048, 16384], P(('groups', 'samp'), 'par'), parts along dimension 0, may hold values from -20 to 20
Outputs:
- gram: float32 [2048, 1024], P(('groups', 'samp'), 'par'), parts along dimension 0
There are 2 independent parts, one for each index of `groups`. A program takes and returns all parts, laid end to end along the dimension named above; each array names one. Nothing has to cross between parts.
All inputs are finite; a program needn't handle non-finite values.
Results may differ from a plain program's by a relative error of at most 0.00005.
Values sent between devices are 32-bit elements; how exact they have to be, the bound alone decides.
A program may use at most 64 MiB of HBM per device.

v0:
```python
import jax
import jax.numpy as jnp
from jax import lax
from jax.sharding import PartitionSpec as P


def passed_along(block, axis, distance):
    devices = range(lax.axis_size(axis))
    route = [((i - distance) % len(devices), i) for i in devices]
    return lax.ppermute(block, axis, route)


def per_device(log_derivs):
    rows = log_derivs.shape[0]
    nsamp = lax.axis_size("samp")
    my_index = lax.axis_index("samp")
    total_rows = rows * nsamp
    highest = lax.Precision.HIGHEST
    col_sums = lax.psum(jnp.sum(log_derivs, axis=0), "samp")
    means = col_sums / total_rows
    source = log_derivs - means[None, :]

    def pair_tile(visit):
        return jnp.dot(source, visit.T, precision=highest, preferred_element_type=jnp.float32)

    start_terms = jnp.zeros((rows, nsamp * rows), jnp.float32)
    start_terms = lax.dynamic_update_slice(
        start_terms, pair_tile(source), (jnp.int32(0), my_index * rows)
    )

    def visit_step(step, carry):
        current, terms_now = carry
        current = passed_along(current, "samp", 1)
        slot = (my_index - step) % nsamp
        terms_now = lax.dynamic_update_slice(
            terms_now, pair_tile(current), (jnp.int32(0), slot * rows)
        )
        return (current, terms_now)

    unused, terms = lax.fori_loop(1, nsamp, visit_step, (source, start_terms))
    gram_share = lax.psum_scatter(terms, "par", scatter_dimension=1, tiled=True)
    return gram_share / total_rows


def solution(mesh):
    in_specs = (P(("groups", "samp"), "par"),)
    out_specs = P(("groups", "samp"), "par")
    return jax.shard_map(
        per_device, mesh=mesh, in_specs=in_specs, out_specs=out_specs, check_vma=False
    )
```

profile of v0, /device:TPU:3, one launch (start us, length us, event | category | flops | bytes accessed | tf_op | source)
XLA Modules:
  0.0 251.7 jit_solution(11880702368004512008)
XLA Ops:
  6.5 2.4 reduce_sum.9
  8.9 9.7 %psum.7 = f32[4096]{0:T(1024)S(1)} all-reduce(f32[4096]{0:T(1024)S(1)} %reduce_sum.9), channel_id=1, replica_groups=mesh['groups'=2,'samp'=4,'par'=4] {'samp'}, use_global_device_ids=true, to_apply=%region_1.0 | all-reduce | flops 4096 | bytes 32768 | tf_op jit(solution)/shard_map/psum | solution.py:19
  18.7 2.6 %broadcast_subtract_fusion = f32[256,4096]{1,0:T(8,128)S(1)} fusion(f32[256,4096]{1,0:T(8,128)} %param.3, f32[4096]{0:T(1024)S(1)} %broadcast_multiply_fusion.1), kind=kLoop, calls=%fused_computation.1 | loop fusion | flops 1048576 | bytes 8404992 | tf_op jit(solution)/shard_map/sub | solution.py:21
  21.4 1.9 copy-done
  23.3 2.0 copy.5
  25.2 0.1 broadcast_in_dim.4
  25.4 11.9 %convolution_dynamic-update-slice_fusion.1 = f32[256,1024]{1,0:T(8,128)S(1)} fusion(f32[256,1024]{1,0:T(8,128)S(1)} %broadcast_in_dim.4, s32[]{:T(128)S(6)} %select_n.33, f32[256,4096]{1,0:T(8,128)} %copy-done), kind=kOutput, calls=%fused_computation.2 | convolution fusion | flops 3221225472 | bytes 8650756 | tf_op jit(solution)/shard_map/dot_general | solution.py:24
  37.3 175.7 %while.17 = (s32[]{:T(128)}, f32[256,4096]{1,0:T(8,128)}, f32[256,1024]{1,0:T(8,128)S(1)}, f32[256,4096]{1,0:T(8,128)}, s32[]{:T(128)}, /*index=5*/s32[]{:T(128)...) while((s32[]{:T(128)}, f32[256,4096]{1,0:T(8,128)}, f32[256,1024]{1,0:T(8,128)S(1)}, ...), condition=%wide.region_3.4_spmd, body=%wide.region_2.3_spmd.sunk | while | flops 3221225472 | bytes 50594132 | solution.py:40
  37.3 2.3 collective-permute-start
  39.6 45.8 %collective-permute-done = f32[256,4096]{1,0:T(8,128)} collective-permute-done((f32[256,4096]{1,0:T(8,128)}, f32[256,4096]{1,0:T(8,128)}, u32[]{:S(2)}, u32[]{:S(2)}) %collective-permute-start) | collective-permute-done | bytes 4194336 | tf_op jit(solution)/shard_map/while/body/eval_jaxpr/ppermute | solution.py:10
  85.4 4.6 %copy.11 = f32[256,4096]{1,0:T(8,128)} copy(f32[256,4096]{1,0:T(8,128)} %collective-permute-done) | data formatting | bytes 8388608 | tf_op jit(solution)/shard_map/while
  90.0 5.7 %convolution_dynamic-update-slice_fusion.3 = f32[256,1024]{1,0:T(8,128)S(1)} fusion(f32[256,1024]{1,0:T(8,128)S(1)} %get-tuple-element.193, s32[]{:T(128)S(6)} %select_n.37, f32[256,4096]{1,0:T(8,128)S(1)} %copy-done.1, f32[256,4096]{1,0:T(8,128)} %collective-permute-done), kind=kOutput, calls=%fused_computation.clone.1 | convolution fusion | flops 3221225472 | bytes 8650756 | tf_op jit(solution)/shard_map/while/body/eval_jaxpr/dot_general | solution.py:24
  95.7 2.5 %collective-permute-start = (f32[256,4096]{1,0:T(8,128)}, f32[256,4096]{1,0:T(8,128)}, u32[]{:S(2)}, u32[]{:S(2)}) collective-permute-start(f32[256,4096]{1,0:T(8,128)} %get-tuple-element.192), channel_id=1, source_target_pairs={{12,0},{0,4},{4,8},{8,12},{13,1},{1,5},{5,9},{9,13},{14,2},{2,6},{... | collective-permute-start | bytes 12582920 | tf_op jit(solution)/shard_map/while/body/eval_jaxpr/ppermute | solution.py:10
  98.3 45.8 %collective-permute-done = f32[256,4096]{1,0:T(8,128)} collective-permute-done((f32[256,4096]{1,0:T(8,128)}, f32[256,4096]{1,0:T(8,128)}, u32[]{:S(2)}, u32[]{:S(2)}) %collective-permute-start) | collective-permute-done | bytes 4194336 | tf_op jit(solution)/shard_map/while/body/eval_jaxpr/ppermute | solution.py:10
  144.0 4.6 %copy.11 = f32[256,4096]{1,0:T(8,128)} copy(f32[256,4096]{1,0:T(8,128)} %collective-permute-done) | data formatting | bytes 8388608 | tf_op jit(solution)/shard_map/while
  148.7 5.7 %convolution_dynamic-update-slice_fusion.3 = f32[256,1024]{1,0:T(8,128)S(1)} fusion(f32[256,1024]{1,0:T(8,128)S(1)} %get-tuple-element.193, s32[]{:T(128)S(6)} %select_n.37, f32[256,4096]{1,0:T(8,128)S(1)} %copy-done.1, f32[256,4096]{1,0:T(8,128)} %collective-permute-done), kind=kOutput, calls=%fused_computation.clone.1 | convolution fusion | flops 3221225472 | bytes 8650756 | tf_op jit(solution)/shard_map/while/body/eval_jaxpr/dot_general | solution.py:24
  154.4 2.5 %collective-permute-start = (f32[256,4096]{1,0:T(8,128)}, f32[256,4096]{1,0:T(8,128)}, u32[]{:S(2)}, u32[]{:S(2)}) collective-permute-start(f32[256,4096]{1,0:T(8,128)} %get-tuple-element.192), channel_id=1, source_target_pairs={{12,0},{0,4},{4,8},{8,12},{13,1},{1,5},{5,9},{9,13},{14,2},{2,6},{... | collective-permute-start | bytes 12582920 | tf_op jit(solution)/shard_map/while/body/eval_jaxpr/ppermute | solution.py:10
  156.9 45.8 %collective-permute-done = f32[256,4096]{1,0:T(8,128)} collective-permute-done((f32[256,4096]{1,0:T(8,128)}, f32[256,4096]{1,0:T(8,128)}, u32[]{:S(2)}, u32[]{:S(2)}) %collective-permute-start) | collective-permute-done | bytes 4194336 | tf_op jit(solution)/shard_map/while/body/eval_jaxpr/ppermute | solution.py:10
  202.7 4.6 %copy.11 = f32[256,4096]{1,0:T(8,128)} copy(f32[256,4096]{1,0:T(8,128)} %collective-permute-done) | data formatting | bytes 8388608 | tf_op jit(solution)/shard_map/while
  207.3 5.7 %convolution_dynamic-update-slice_fusion.3 = f32[256,1024]{1,0:T(8,128)S(1)} fusion(f32[256,1024]{1,0:T(8,128)S(1)} %get-tuple-element.193, s32[]{:T(128)S(6)} %select_n.37, f32[256,4096]{1,0:T(8,128)S(1)} %copy-done.1, f32[256,4096]{1,0:T(8,128)} %collective-permute-done), kind=kOutput, calls=%fused_computation.clone.1 | convolution fusion | flops 3221225472 | bytes 8650756 | tf_op jit(solution)/shard_map/while/body/eval_jaxpr/dot_general | solution.py:24
  213.1 1.0 copy-done.2
  214.0 0.0 reduce-scatter.2.cloned.1.call-update
  214.1 29.1 %reduce-scatter.2.cloned.1.call-done = f32[256,256]{1,0:T(8,128)} async-done(((f32[256,1024]{1,0:T(8,128)}), f32[256,256]{1,0:T(8,128)}) %reduce-scatter.2.cloned.1.call-update) | async-done | bytes 262160 | tf_op jit(solution)/shard_map/reduce_scatter | solution.py:41
  243.2 1.7 broadcast_multiply_fusion
  (10 shorter events, 0.0 us)
Async XLA Ops:
  6.5 236.6 %reduce-scatter.2.cloned.1.call-start = ((), (), s32[]{:S(2)}) async-start(), calls=%async_computation.1 | async-start | bytes 1310720 | tf_op jit(solution)/shard_map/reduce_scatter | solution.py:41
  21.3 1.9 copy-start
  37.3 48.1 %collective-permute-start = (f32[256,4096]{1,0:T(8,128)}, f32[256,4096]{1,0:T(8,128)}, u32[]{:S(2)}, u32[]{:S(2)}) collective-permute-start(f32[256,4096]{1,0:T(8,128)} %get-tuple-element.192), channel_id=1, source_target_pairs={{12,0},{0,4},{4,8},{8,12},{13,1},{1,5},{5,9},{9,13},{14,2},{2,6},{... | collective-permute-start | bytes 12582920 | tf_op jit(solution)/shard_map/while/body/eval_jaxpr/ppermute | solution.py:10
  39.6 50.4 %copy-start.1 = (f32[256,4096]{1,0:T(8,128)S(1)}, f32[256,4096]{1,0:T(8,128)}, u32[]{:S(2)}) copy-start(f32[256,4096]{1,0:T(8,128)} %get-tuple-element.205) | copy-start | bytes 12582916 | tf_op jit(solution)/shard_map/while
  95.7 48.3 %collective-permute-start = (f32[256,4096]{1,0:T(8,128)}, f32[256,4096]{1,0:T(8,128)}, u32[]{:S(2)}, u32[]{:S(2)}) collective-permute-start(f32[256,4096]{1,0:T(8,128)} %get-tuple-element.192), channel_id=1, source_target_pairs={{12,0},{0,4},{4,8},{8,12},{13,1},{1,5},{5,9},{9,13},{14,2},{2,6},{... | collective-permute-start | bytes 12582920 | tf_op jit(solution)/shard_map/while/body/eval_jaxpr/ppermute | solution.py:10
  98.3 50.4 %copy-start.1 = (f32[256,4096]{1,0:T(8,128)S(1)}, f32[256,4096]{1,0:T(8,128)}, u32[]{:S(2)}) copy-start(f32[256,4096]{1,0:T(8,128)} %get-tuple-element.205) | copy-start | bytes 12582916 | tf_op jit(solution)/shard_map/while
  154.4 48.3 %collective-permute-start = (f32[256,4096]{1,0:T(8,128)}, f32[256,4096]{1,0:T(8,128)}, u32[]{:S(2)}, u32[]{:S(2)}) collective-permute-start(f32[256,4096]{1,0:T(8,128)} %get-tuple-element.192), channel_id=1, source_target_pairs={{12,0},{0,4},{4,8},{8,12},{13,1},{1,5},{5,9},{9,13},{14,2},{2,6},{... | collective-permute-start | bytes 12582920 | tf_op jit(solution)/shard_map/while/body/eval_jaxpr/ppermute | solution.py:10
  156.9 50.4 %copy-start.1 = (f32[256,4096]{1,0:T(8,128)S(1)}, f32[256,4096]{1,0:T(8,128)}, u32[]{:S(2)}) copy-start(f32[256,4096]{1,0:T(8,128)} %get-tuple-element.205) | copy-start | bytes 12582916 | tf_op jit(solution)/shard_map/while
  213.1 1.0 copy-start.2
Sparse Core Ops, SparseCore 0:
  214.2 28.9 reduce-scatter.1
where the time goes:
time: 254 us; the launch traced here: 252 us
  waiting for transfers between devices  166 us (65%)
  matrix products  29.1 us (11%)
  local copies, waits for them, and re-layouts  18.8 us (7%)
  between operations  13.4 us (5%)
  blocking collectives  9.75 us (4%)
  starting transfers between devices  7.39 us (3%)
  other arithmetic  6.72 us (3%)
    ppermute x3, waiting for transfers between devices, passed_along(): return lax.ppermute(block, axis, route)  137 us
    reduce_scatter x1, waiting for transfers between devices, per_device(): gram_share = lax.psum_scatter(terms, 'par', scatter_dimension=1, tiled=True)  29.1 us
    dot_general x4, matrix products, pair_tile(): jnp.dot(source, visit.T, precision=highest, preferred_element_type=jnp.fl...  29.1 us
    while x9, local copies, waits for them, and re-layouts  13.9 us
    psum x1, blocking collectives, per_device(): col_sums = lax.psum(jnp.sum(log_derivs, axis=0), 'samp')  9.75 us
    ppermute x3, starting transfers between devices, passed_along(): return lax.ppermute(block, axis, route)  7.39 us
  transfers between devices with their start and end apart: 4, of which 4 were waited for; matrix products, arithmetic and copies ran while one was open for 0% of the time, Pallas kernels for 0%

commit v1 on v0

v1 whole, which is shorter than its diff:
```python
import functools

import jax
import jax.numpy as jnp
from jax import lax
from jax.experimental import pallas as pl
from jax.experimental.pallas import tpu as pltpu
from jax.sharding import PartitionSpec as P

MESH = pl.DeviceIdType.MESH


def split(value):
    high = value.astype(jnp.bfloat16)
    low = (value - high.astype(jnp.float32)).astype(jnp.bfloat16)
    return high, low


def dot_nt(a, b):
    return lax.dot_general(a, b, (((1,), (1,)), ((), ())), preferred_element_type=jnp.float32)


def dot_split(a_high, a_low, b_high, b_low):
    return dot_nt(a_high, b_high) + (dot_nt(a_high, b_low) + dot_nt(a_low, b_high))


def kernel(nsamp, npar, pieces, x_ref, out_ref, own, mate, raw, sums, mean, high, low, terms, arrived,
           total, mirrored, load_sem, sum_send, sum_recv, mate_send, mate_recv, raw_send, raw_recv,
           fwd_send, fwd_recv, z_send, z_recv, mir_send, mir_recv):
    rows, cols = own.shape
    half = cols // 2
    chips = nsamp // 2
    piece = rows // pieces
    total_rows = rows * nsamp
    items = (chips - 1) * pieces
    me = lax.axis_index("samp")
    z = lax.axis_index("par")
    chip = me // 2
    core = me % 2
    other = chip * 2 + (1 - core)
    block_chip = z // 2
    block_distance = (block_chip - chip + chips) % chips
    crosses = block_distance != 0

    load = pltpu.make_async_copy(x_ref, own, load_sem)
    load.start()

    barrier = pltpu.get_barrier_semaphore()
    for step in range(1, nsamp):
        pl.semaphore_signal(barrier, inc=1, device_id={"samp": (me + step) % nsamp}, device_id_type=MESH)
    for step in range(1, npar):
        pl.semaphore_signal(barrier, inc=1, device_id={"par": (z + step) % npar}, device_id_type=MESH)

    @pl.when(crosses)
    def _():
        pl.semaphore_signal(barrier, inc=1, device_id={"samp": z, "par": me}, device_id_type=MESH)

    pl.semaphore_wait(barrier, nsamp + npar - 2 + jnp.where(crosses, 1, 0))

    def piece_rows(k):
        return pl.ds(pl.multiple_of(k * piece, piece), piece)

    def raw_copy(d, k):
        there = (chip + d) % chips
        begin = pl.multiple_of(jnp.where(there < chip, 0, half), 128)
        slot = chips - 1 - d
        return pltpu.make_async_remote_copy(
            src_ref=x_ref.at[piece_rows(k), pl.ds(begin, half)],
            dst_ref=raw.at[slot, core, piece_rows(k)],
            send_sem=raw_send.at[d - 1, k],
            recv_sem=raw_recv.at[slot, k],
            device_id={"samp": there * 2 + core},
            device_id_type=MESH,
        )

    def raw_landed(d, k):
        return pltpu.make_async_remote_copy(
            src_ref=x_ref.at[piece_rows(k), pl.ds(0, half)],
            dst_ref=raw.at[d - 1, core, piece_rows(k)],
            send_sem=raw_send.at[d - 1, k],
            recv_sem=raw_recv.at[d - 1, k],
            device_id={"samp": other},
            device_id_type=MESH,
        )

    def fwd_copy(d, k, which):
        return pltpu.make_async_remote_copy(
            src_ref=raw.at[d - 1, which, piece_rows(k)],
            dst_ref=raw.at[d - 1, which, piece_rows(k)],
            send_sem=fwd_send.at[d - 1, k],
            recv_sem=fwd_recv.at[d - 1, k],
            device_id={"samp": other},
            device_id_type=MESH,
        )

    def sum_copy(source, target):
        return pltpu.make_async_remote_copy(
            src_ref=sums.at[source],
            dst_ref=sums.at[source],
            send_sem=sum_send.at[target],
            recv_sem=sum_recv.at[source],
            device_id={"samp": target},
            device_id_type=MESH,
        )

    mate_copy = pltpu.make_async_remote_copy(
        src_ref=x_ref,
        dst_ref=mate,
        send_sem=mate_send,
        recv_sem=mate_recv,
        device_id={"samp": other},
        device_id_type=MESH,
    )

    def z_copy(block, sender, target, where, k):
        return pltpu.make_async_remote_copy(
            src_ref=terms.at[block, where],
            dst_ref=arrived.at[sender, where],
            send_sem=z_send.at[block, k],
            recv_sem=z_recv.at[sender, k],
            device_id={"par": target},
            device_id_type=MESH,
        )

    def mirror_copy(k):
        return pltpu.make_async_remote_copy(
            src_ref=total.at[piece_rows(k)],
            dst_ref=mirrored.at[piece_rows(k)],
            send_sem=mir_send.at[k],
            recv_sem=mir_recv.at[k],
            device_id={"samp": z, "par": me},
            device_id_type=MESH,
        )

    everything = pl.ds(0, rows)

    for d in range(1, chips):
        raw_copy(d, 0).start()
    load.wait()

    def add_rows(i, acc):
        return acc + own[pl.ds(pl.multiple_of(i * 8, 8), 8), :]

    acc = lax.fori_loop(1, rows // 8, add_rows, own[pl.ds(0, 8), :])
    sums[me] = jnp.sum(acc, axis=0, keepdims=True)
    for step in range(1, nsamp):
        sum_copy(me, (me + step) % nsamp).start()
    mate_copy.start()

    @pl.loop(0, chips - 1)
    def _(i):
        @pl.loop(1, pieces)
        def _(k):
            raw_copy(i + 1, k).start()

    for step in range(1, nsamp):
        sum_copy((me + step) % nsamp, me).wait_recv()
    col_sum = sums[0]
    for s in range(1, nsamp):
        col_sum = col_sum + sums[s]
    mean[...] = col_sum / total_rows

    @pl.loop(0, rows // 16)
    def _(i):
        at = pl.ds(pl.multiple_of(i * 16, 16), 16)
        h, l = split(own[at, :] - mean[...])
        high[at, :] = h
        low[at, :] = l

    width = min(512, cols)

    def send_block(block, where, k):
        @pl.when(block != z)
        def _():
            z_copy(block, z, block, where, k).start()

        @pl.when(block == z)
        def _():
            arrived[z, where] = terms[block, where]

    terms[me] = jnp.zeros((rows, rows), jnp.float32)

    @pl.loop(0, cols // width)
    def _(i):
        at = pl.ds(pl.multiple_of(i * width, width), width)
        h = high[:, at]
        l = low[:, at]
        terms[me] += dot_split(h, l, h, l)

    send_block(me, everything, 0)
    terms[other] = jnp.zeros((rows, rows), jnp.float32)
    mate_copy.wait_recv()

    @pl.loop(0, cols // width)
    def _(i):
        at = pl.ds(pl.multiple_of(i * width, width), width)
        h, l = split(mate[:, at] - mean[:, at])
        terms[other] += dot_split(h, l, high[:, at], low[:, at])

    send_block(other, everything, 0)

    def chunk_term(d, k, which):
        there = (chip + d) % chips
        begin = pl.multiple_of(jnp.where(chip < there, 0, half), 128)
        at = pl.ds(begin, half)
        h, l = split(raw[d - 1, which, piece_rows(k)] - mean[:, at])
        block = there * 2 + which
        terms[block, piece_rows(k)] = dot_split(h, l, high[:, at], low[:, at])
        send_block(block, piece_rows(k), k)

    def gather_sum(k):
        where = piece_rows(k)
        for step in range(1, npar):
            z_copy(z, (z + step) % npar, z, where, k).wait_recv()
        value = arrived[0, where]
        for s in range(1, npar):
            value = value + arrived[s, where]
        total[where] = value
        mirror_copy(k).start()

    def gather_item(j):
        @pl.when(crosses & (j // pieces + 1 == block_distance))
        def _():
            gather_sum(j % pieces)

    @pl.loop(0, items)
    def _(j):
        d = j // pieces + 1
        k = j % pieces
        raw_landed(d, k).wait_recv()
        fwd_copy(d, k, core).start()
        chunk_term(d, k, core)
        fwd_copy(d, k, 1 - core).wait_recv()
        chunk_term(d, k, 1 - core)

        @pl.when(j > 0)
        def _():
            gather_item(j - 1)

    gather_item(items - 1)

    @pl.when(jnp.logical_not(crosses))
    def _():
        for step in range(1, npar):
            z_copy(z, (z + step) % npar, z, everything, 0).wait_recv()
        value = arrived[0]
        for s in range(1, npar):
            value = value + arrived[s]
        out_ref[...] = value.T / total_rows

    @pl.when(crosses)
    def _():
        flipped = total[...].T

        @pl.loop(0, pieces)
        def _(k):
            mirror_copy(k).wait_recv()

        out_ref[...] = (flipped + mirrored[...]) / total_rows

        @pl.loop(0, pieces)
        def _(k):
            mirror_copy(k).wait_send()

    for step in range(1, nsamp):
        sum_copy(me, (me + step) % nsamp).wait_send()
    mate_copy.wait_send()

    @pl.loop(0, items)
    def _(j):
        d = j // pieces + 1
        k = j % pieces
        raw_copy(d, k).wait_send()
        fwd_copy(d, k, core).wait_send()
        for which in range(2):
            block = ((chip + d) % chips) * 2 + which

            @pl.when(block != z)
            def _():
                z_copy(block, z, block, piece_rows(k), k).wait_send()

    for block in (me, other):
        @pl.when(block != z)
        def _():
            z_copy(block, z, block, everything, 0).wait_send()


def per_device(nsamp, npar, log_derivs):
    rows, cols = log_derivs.shape
    pieces = 8
    chips = nsamp // 2
    dma = pltpu.SemaphoreType.DMA
    f32, bf16 = jnp.float32, jnp.bfloat16
    return pl.pallas_call(
        functools.partial(kernel, nsamp, npar, pieces),
        out_shape=jax.ShapeDtypeStruct((rows, rows), f32),
        in_specs=[pl.BlockSpec(memory_space=pl.ANY)],
        out_specs=pl.BlockSpec(memory_space=pltpu.VMEM),
        scratch_shapes=[
            pltpu.VMEM((rows, cols), f32),
            pltpu.VMEM((rows, cols), f32),
            pltpu.VMEM((chips - 1, 2, rows, cols // 2), f32),
            pltpu.VMEM((nsamp, 1, cols), f32),
            pltpu.VMEM((1, cols), f32),
            pltpu.VMEM((rows, cols), bf16),
            pltpu.VMEM((rows, cols), bf16),
            pltpu.VMEM((nsamp, rows, rows), f32),
            pltpu.VMEM((npar, rows, rows), f32),
            pltpu.VMEM((rows, rows), f32),
            pltpu.VMEM((rows, rows), f32),
            dma,
            dma((nsamp,)),
            dma((nsamp,)),
            dma,
            dma,
            dma((chips - 1, pieces)),
            dma((chips - 1, pieces)),
            dma((chips - 1, pieces)),
            dma((chips - 1, pieces)),
            dma((nsamp, pieces)),
            dma((npar, pieces)),
            dma((pieces,)),
            dma((pieces,)),
        ],
        compiler_params=pltpu.CompilerParams(
            collective_id=0, has_side_effects=True, vmem_limit_bytes=48 * 1024 * 1024
        ),
    )(log_derivs)


def solution(mesh):
    nsamp, npar = mesh.shape["samp"], mesh.shape["par"]
    spec = P(("groups", "samp"), "par")
    return jax.shard_map(
        functools.partial(per_device, nsamp, npar),
        mesh=mesh, in_specs=(spec,), out_specs=spec, check_vma=False,
    )
```

time: 254 us -> 68.6 us (0.27)
  waiting for transfers between devices: 166 us -> 0 us
  Pallas kernels: 0 us -> 65.6 us
  matrix products: 29.1 us -> 0 us
  local copies, waits for them, and re-layouts: 18.8 us -> 2.89 us
  between operations: 13.4 us -> 0.01 us
  blocking collectives: 9.75 us -> 0 us
  starting transfers between devices: 7.39 us -> 0 us
  other arithmetic: 6.72 us -> 0 us
    ppermute x3 -> x0, waiting for transfers between devices: 137 us -> none  [passed_along(): return lax.ppermute(block, axis, route)]
    pallas_call x0 -> x1, Pallas kernels: none -> 65.6 us  [per_device(): pl.pallas_call(functools.partial(kernel, nsamp, npar, pieces), out_shape=...]
    reduce_scatter x1 -> x0, waiting for transfers between devices: 29.1 us -> none  [per_device(): gram_share = lax.psum_scatter(terms, 'par', scatter_dimension=1, tiled=True)]
    dot_general x4 -> x0, matrix products: 29.1 us -> none  [pair_tile(): jnp.dot(source, visit.T, precision=highest, preferred_element_type=jnp.fl...]
    while x9 -> x0, local copies, waits for them, and re-layouts: 13.9 us -> none
    psum x1 -> x0, blocking collectives: 9.75 us -> none  [per_device(): col_sums = lax.psum(jnp.sum(log_derivs, axis=0), 'samp')]
    ppermute x3 -> x0, starting transfers between devices: 7.39 us -> none  [passed_along(): return lax.ppermute(block, axis, route)]
    sub x1 -> x0, other arithmetic: 2.65 us -> none  [per_device(): source = log_derivs - means[None, :]]
  transfers between devices with their start and end apart: 4 -> 0, of which waited for: 4 -> 0; matrix products, arithmetic and copies ran while one was open for 0% -> 0% of each run, Pallas kernels for 0% -> 0%
where the time goes in v1:
time: 68.6 us; the launch traced here: 68.5 us
  Pallas kernels  65.6 us (96%)
  local copies, waits for them, and re-layouts  2.89 us (4%)
    pallas_call x1, Pallas kernels, per_device(): pl.pallas_call(functools.partial(kernel, nsamp, npar, pieces), out_shape=...  65.6 us
    unnamed x3, local copies, waits for them, and re-layouts  2.89 us

profile of v1, /device:TPU:3, one launch (start us, length us, event | category | flops | bytes accessed | tf_op | source)
XLA Modules:
  0.0 68.5 jit_solution(2333819391519802245)
XLA Ops:
  0.0 0.0 copy-start
  0.0 2.2 %copy-done = f32[256,4096]{1,0:T(8,128)S(1)} copy-done((f32[256,4096]{1,0:T(8,128)S(1)}, f32[256,4096]{1,0:T(8,128)}, u32[]{:S(2)}) %copy-start) | copy-done | bytes 4194328
  2.2 65.6 %shard_map.17 = f32[256,256]{1,0:T(8,128)S(1)} custom-call(f32[256,4096]{1,0:T(8,128)S(1)} %copy-done), custom_call_target="tpu_custom_call" | custom-call | tf_op jit(solution)/shard_map/pallas_call | solution.py:294
  67.8 0.7 %copy.3 = f32[256,256]{1,0:T(8,128)} copy(f32[256,256]{1,0:T(8,128)S(1)} %shard_map.17) | data formatting | bytes 524288
Async XLA Ops:
  0.0 2.2 %copy-start = (f32[256,4096]{1,0:T(8,128)S(1)}, f32[256,4096]{1,0:T(8,128)}, u32[]{:S(2)}) copy-start(f32[256,4096]{1,0:T(8,128)} %x_ref.1) | copy-start | bytes 12582916

commit v2 on v1

--- a/solution.py
+++ b/solution.py
@@ -8,6 +8,7 @@
 from jax.sharding import PartitionSpec as P
 
 MESH = pl.DeviceIdType.MESH
+FLIP = False
 
 
 def split(value):
@@ -24,15 +25,16 @@
     return dot_nt(a_high, b_high) + (dot_nt(a_high, b_low) + dot_nt(a_low, b_high))
 
 
-def kernel(nsamp, npar, pieces, x_ref, out_ref, own, mate, raw, sums, mean, high, low, terms, arrived,
+def kernel(nsamp, npar, sizes, x_ref, out_ref, own, mate, raw, middle, sums, mean, high, low, terms, arrived,
            total, mirrored, load_sem, sum_send, sum_recv, mate_send, mate_recv, raw_send, raw_recv,
-           fwd_send, fwd_recv, z_send, z_recv, mir_send, mir_recv):
+           fwd_send, fwd_recv, mid_send, mid_recv, midfwd_send, midfwd_recv, z_send, z_recv, mir_send, mir_recv):
     rows, cols = own.shape
-    half = cols // 2
+    span = raw.shape[3]
+    spare = cols - 2 * span
     chips = nsamp // 2
-    piece = rows // pieces
+    pieces = len(sizes)
+    starts = [sum(sizes[:k]) for k in range(pieces)]
     total_rows = rows * nsamp
-    items = (chips - 1) * pieces
     me = lax.axis_index("samp")
     z = lax.axis_index("par")
     chip = me // 2
@@ -58,14 +60,21 @@
     pl.semaphore_wait(barrier, nsamp + npar - 2 + jnp.where(crosses, 1, 0))
 
     def piece_rows(k):
-        return pl.ds(pl.multiple_of(k * piece, piece), piece)
+        return pl.ds(starts[k], sizes[k])
+
+    def lower_takes_middle(low_chip, high_chip):
+        return (z // 2 != low_chip) if FLIP else (z // 2 == low_chip)
+
+    def takes_middle(taker, giver):
+        lower = jnp.minimum(taker, giver)
+        return lower_takes_middle(lower, jnp.maximum(taker, giver)) == (taker == lower)
 
     def raw_copy(d, k):
         there = (chip + d) % chips
-        begin = pl.multiple_of(jnp.where(there < chip, 0, half), 128)
+        begin = pl.multiple_of(jnp.where(there < chip, 0, cols - span), 128)
         slot = chips - 1 - d
         return pltpu.make_async_remote_copy(
-            src_ref=x_ref.at[piece_rows(k), pl.ds(begin, half)],
+            src_ref=x_ref.at[piece_rows(k), pl.ds(begin, span)],
             dst_ref=raw.at[slot, core, piece_rows(k)],
             send_sem=raw_send.at[d - 1, k],
             recv_sem=raw_recv.at[slot, k],
@@ -75,7 +84,7 @@
 
     def raw_landed(d, k):
         return pltpu.make_async_remote_copy(
-            src_ref=x_ref.at[piece_rows(k), pl.ds(0, half)],
+            src_ref=x_ref.at[piece_rows(k), pl.ds(0, span)],
             dst_ref=raw.at[d - 1, core, piece_rows(k)],
             send_sem=raw_send.at[d - 1, k],
             recv_sem=raw_recv.at[d - 1, k],
@@ -89,6 +98,38 @@
             dst_ref=raw.at[d - 1, which, piece_rows(k)],
             send_sem=fwd_send.at[d - 1, k],
             recv_sem=fwd_recv.at[d - 1, k],
+            device_id={"samp": other},
+            device_id_type=MESH,
+        )
+
+    def mid_copy(d):
+        there = (chip + d) % chips
+        slot = chips - 1 - d
+        return pltpu.make_async_remote_copy(
+            src_ref=x_ref.at[:, pl.ds(span, spare)],
+            dst_ref=middle.at[slot, core],
+            send_sem=mid_send.at[d - 1],
+            recv_sem=mid_recv.at[slot],
+            device_id={"samp": there * 2 + core},
+            device_id_type=MESH,
+        )
+
+    def mid_landed(d):
+        return pltpu.make_async_remote_copy(
+            src_ref=x_ref.at[:, pl.ds(span, spare)],
+            dst_ref=middle.at[d - 1, core],
+            send_sem=mid_send.at[d - 1],
+            recv_sem=mid_recv.at[d - 1],
+            device_id={"samp": other},
+            device_id_type=MESH,
+        )
+
+    def midfwd_copy(d, which):
+        return pltpu.make_async_remote_copy(
+            src_ref=middle.at[d - 1, which],
+            dst_ref=middle.at[d - 1, which],
+            send_sem=midfwd_send.at[d - 1],
+            recv_sem=midfwd_recv.at[d - 1],
             device_id={"samp": other},
             device_id_type=MESH,
         )
@@ -135,6 +176,10 @@
     everything = pl.ds(0, rows)
 
     for d in range(1, chips):
+        @pl.when(takes_middle((chip + d) % chips, chip))
+        def _():
+            mid_copy(d).start()
+
         raw_copy(d, 0).start()
     load.wait()
 
@@ -147,11 +192,10 @@
         sum_copy(me, (me + step) % nsamp).start()
     mate_copy.start()
 
-    @pl.loop(0, chips - 1)
-    def _(i):
-        @pl.loop(1, pieces)
-        def _(k):
-            raw_copy(i + 1, k).start()
+    @pl.loop(1, chips)
+    def _(d):
+        for k in range(1, pieces):
+            raw_copy(d, k).start()
 
     for step in range(1, nsamp):
         sum_copy((me + step) % nsamp, me).wait_recv()
@@ -199,14 +243,39 @@
 
     send_block(other, everything, 0)
 
-    def chunk_term(d, k, which):
+    def first_terms(d):
         there = (chip + d) % chips
-        begin = pl.multiple_of(jnp.where(chip < there, 0, half), 128)
-        at = pl.ds(begin, half)
-        h, l = split(raw[d - 1, which, piece_rows(k)] - mean[:, at])
-        block = there * 2 + which
-        terms[block, piece_rows(k)] = dot_split(h, l, high[:, at], low[:, at])
-        send_block(block, piece_rows(k), k)
+        takes = takes_middle(chip, there)
+
+        @pl.when(takes)
+        def _():
+            at = pl.ds(span, spare)
+            mid_landed(d).wait_recv()
+            midfwd_copy(d, core).start()
+            midfwd_copy(d, 1 - core).wait_recv()
+            for which in range(2):
+                h, l = split(middle[d - 1, which] - mean[:, at])
+                terms[there * 2 + which] = dot_split(h, l, high[:, at], low[:, at])
+
+        @pl.when(jnp.logical_not(takes))
+        def _():
+            for which in range(2):
+                terms[there * 2 + which] = jnp.zeros((rows, rows), jnp.float32)
+
+    def chunk_terms(d, k):
+        there = (chip + d) % chips
+        begin = pl.multiple_of(jnp.where(chip < there, 0, cols - span), 128)
+        at = pl.ds(begin, span)
+        where = piece_rows(k)
+        size = sizes[k]
+        both = jnp.concatenate([raw[d - 1, 0, where], raw[d - 1, 1, where]], axis=0) - mean[:, at]
+        h, l = split(both)
+        stacked = dot_nt(jnp.concatenate([h, l], axis=0), high[:, at])
+        value = stacked[:2 * size] + (stacked[2 * size:] + dot_nt(h, low[:, at]))
+        for which in range(2):
+            block = there * 2 + which
+            terms[block, where] += value[which * size:(which + 1) * size]
+            send_block(block, where, k)
 
     def gather_sum(k):
         where = piece_rows(k)
@@ -218,26 +287,22 @@
         total[where] = value
         mirror_copy(k).start()
 
-    def gather_item(j):
-        @pl.when(crosses & (j // pieces + 1 == block_distance))
-        def _():
-            gather_sum(j % pieces)
-
-    @pl.loop(0, items)
-    def _(j):
-        d = j // pieces + 1
-        k = j % pieces
-        raw_landed(d, k).wait_recv()
-        fwd_copy(d, k, core).start()
-        chunk_term(d, k, core)
-        fwd_copy(d, k, 1 - core).wait_recv()
-        chunk_term(d, k, 1 - core)
-
-        @pl.when(j > 0)
-        def _():
-            gather_item(j - 1)
-
-    gather_item(items - 1)
+    def gather_piece(d, k):
+        @pl.when(block_distance == d)
+        def _():
+            gather_sum(k)
+
+    @pl.loop(1, chips)
+    def _(d):
+        first_terms(d)
+        for k in range(pieces):
+            raw_landed(d, k).wait_recv()
+            fwd_copy(d, k, core).start()
+            fwd_copy(d, k, 1 - core).wait_recv()
+            chunk_terms(d, k)
+            if k > 0:
+                gather_piece(d, k - 1)
+        gather_piece(d, pieces - 1)
 
     @pl.when(jnp.logical_not(crosses))
     def _():
@@ -252,32 +317,38 @@
     def _():
         flipped = total[...].T
 
-        @pl.loop(0, pieces)
-        def _(k):
+        for k in range(pieces):
             mirror_copy(k).wait_recv()
-
-        out_ref[...] = (flipped + mirrored[...]) / total_rows
-
-        @pl.loop(0, pieces)
-        def _(k):
+            where = piece_rows(k)
+            out_ref[where] = (flipped[starts[k]:starts[k] + sizes[k]] + mirrored[where]) / total_rows
+        for k in range(pieces):
             mirror_copy(k).wait_send()
 
     for step in range(1, nsamp):
         sum_copy(me, (me + step) % nsamp).wait_send()
     mate_copy.wait_send()
 
-    @pl.loop(0, items)
-    def _(j):
-        d = j // pieces + 1
-        k = j % pieces
-        raw_copy(d, k).wait_send()
-        fwd_copy(d, k, core).wait_send()
-        for which in range(2):
-            block = ((chip + d) % chips) * 2 + which
-
-            @pl.when(block != z)
-            def _():
-                z_copy(block, z, block, piece_rows(k), k).wait_send()
+    @pl.loop(1, chips)
+    def _(d):
+        there = (chip + d) % chips
+
+        @pl.when(takes_middle(there, chip))
+        def _():
+            mid_copy(d).wait_send()
+
+        @pl.when(takes_middle(chip, there))
+        def _():
+            midfwd_copy(d, core).wait_send()
+
+        for k in range(pieces):
+            raw_copy(d, k).wait_send()
+            fwd_copy(d, k, core).wait_send()
+            for which in range(2):
+                block = there * 2 + which
+
+                @pl.when(block != z)
+                def _():
+                    z_copy(block, z, block, piece_rows(k), k).wait_send()
 
     for block in (me, other):
         @pl.when(block != z)
@@ -285,21 +356,30 @@
             z_copy(block, z, block, everything, 0).wait_send()
 
 
+def piece_sizes(rows):
+    sizes = [64] * (rows // 64 - 1) + [32]
+    return sizes + [16, 16]
+
+
 def per_device(nsamp, npar, log_derivs):
     rows, cols = log_derivs.shape
-    pieces = 8
+    sizes = piece_sizes(rows)
+    pieces = len(sizes)
+    spare = 256
+    span = (cols - spare) // 2
     chips = nsamp // 2
     dma = pltpu.SemaphoreType.DMA
     f32, bf16 = jnp.float32, jnp.bfloat16
     return pl.pallas_call(
-        functools.partial(kernel, nsamp, npar, pieces),
+        functools.partial(kernel, nsamp, npar, sizes),
         out_shape=jax.ShapeDtypeStruct((rows, rows), f32),
-        in_specs=[pl.BlockSpec(memory_space=pl.ANY)],
+        in_specs=[pl.BlockSpec(memory_space=pltpu.HBM)],
         out_specs=pl.BlockSpec(memory_space=pltpu.VMEM),
         scratch_shapes=[
             pltpu.VMEM((rows, cols), f32),
             pltpu.VMEM((rows, cols), f32),
-            pltpu.VMEM((chips - 1, 2, rows, cols // 2), f32),
+            pltpu.VMEM((chips - 1, 2, rows, span), f32),
+            pltpu.VMEM((chips - 1, 2, rows, spare), f32),
             pltpu.VMEM((nsamp, 1, cols), f32),
             pltpu.VMEM((1, cols), f32),
             pltpu.VMEM((rows, cols), bf16),
@@ -317,6 +397,10 @@
             dma((chips - 1, pieces)),
             dma((chips - 1, pieces)),
             dma((chips - 1, pieces)),
+            dma((chips - 1,)),
+            dma((chips - 1,)),
+            dma((chips - 1,)),
+            dma((chips - 1,)),
             dma((nsamp, pieces)),
             dma((npar, pieces)),
             dma((pieces,)),

time: 68.6 us -> 69.1 us (level)
  no operation moved by 1% of the time
where the time goes in v2:
time: 69.1 us; the launch traced here: 68.6 us
  Pallas kernels  65.7 us (95%)
  local copies, waits for them, and re-layouts  2.89 us (4%)
    pallas_call x1, Pallas kernels, per_device(): pl.pallas_call(functools.partial(kernel, nsamp, npar, sizes), out_shape=j...  65.7 us
    unnamed x3, local copies, waits for them, and re-layouts  2.89 us

profile of v2, /device:TPU:3, one launch (start us, length us, event | category | flops | bytes accessed | tf_op | source)
XLA Modules:
  0.0 68.6 jit_solution(14024726308510164313)
XLA Ops:
  0.0 0.0 copy-start
  0.0 2.2 %copy-done = f32[256,4096]{1,0:T(8,128)S(1)} copy-done((f32[256,4096]{1,0:T(8,128)S(1)}, f32[256,4096]{1,0:T(8,128)}, u32[]{:S(2)}) %copy-start) | copy-done | bytes 4194328
  2.2 65.7 %shard_map.17 = f32[256,256]{1,0:T(8,128)S(1)} custom-call(f32[256,4096]{1,0:T(8,128)S(1)} %copy-done), custom_call_target="tpu_custom_call" | custom-call | tf_op jit(solution)/shard_map/pallas_call | solution.py:373
  67.9 0.7 %copy.3 = f32[256,256]{1,0:T(8,128)} copy(f32[256,256]{1,0:T(8,128)S(1)} %shard_map.17) | data formatting | bytes 524288
Async XLA Ops:
  0.0 2.2 %copy-start = (f32[256,4096]{1,0:T(8,128)S(1)}, f32[256,4096]{1,0:T(8,128)}, u32[]{:S(2)}) copy-start(f32[256,4096]{1,0:T(8,128)} %x_ref.1) | copy-start | bytes 12582916

commit v3 on v1

--- a/solution.py
+++ b/solution.py
@@ -205,7 +205,8 @@
         at = pl.ds(begin, half)
         h, l = split(raw[d - 1, which, piece_rows(k)] - mean[:, at])
         block = there * 2 + which
-        terms[block, piece_rows(k)] = dot_split(h, l, high[:, at], low[:, at])
+        stacked = dot_nt(jnp.concatenate([h, l], axis=0), high[:, at])
+        terms[block, piece_rows(k)] = stacked[:piece] + (stacked[piece:] + dot_nt(h, low[:, at]))
         send_block(block, piece_rows(k), k)
 
     def gather_sum(k):
@@ -294,7 +295,7 @@
     return pl.pallas_call(
         functools.partial(kernel, nsamp, npar, pieces),
         out_shape=jax.ShapeDtypeStruct((rows, rows), f32),
-        in_specs=[pl.BlockSpec(memory_space=pl.ANY)],
+        in_specs=[pl.BlockSpec(memory_space=pltpu.HBM)],
         out_specs=pl.BlockSpec(memory_space=pltpu.VMEM),
         scratch_shapes=[
             pltpu.VMEM((rows, cols), f32),

time: 68.6 us -> 67.6 us (0.985)
  Pallas kernels: 65.6 us -> 64.6 us
    pallas_call x1, Pallas kernels: 65.6 us -> 64.6 us  [per_device(): pl.pallas_call(functools.partial(kernel, nsamp, npar, pieces), out_shape=...]
where the time goes in v3:
time: 67.6 us; the launch traced here: 67.5 us
  Pallas kernels  64.6 us (96%)
  local copies, waits for them, and re-layouts  2.89 us (4%)
    pallas_call x1, Pallas kernels, per_device(): pl.pallas_call(functools.partial(kernel, nsamp, npar, pieces), out_shape=...  64.6 us
    unnamed x3, local copies, waits for them, and re-layouts  2.89 us

profile of v3, /device:TPU:3, one launch (start us, length us, event | category | flops | bytes accessed | tf_op | source)
XLA Modules:
  0.0 67.5 jit_solution(17055361751989430160)
XLA Ops:
  0.0 0.0 copy-start
  0.0 2.2 %copy-done = f32[256,4096]{1,0:T(8,128)S(1)} copy-done((f32[256,4096]{1,0:T(8,128)S(1)}, f32[256,4096]{1,0:T(8,128)}, u32[]{:S(2)}) %copy-start) | copy-done | bytes 4194328
  2.2 64.6 %shard_map.17 = f32[256,256]{1,0:T(8,128)S(1)} custom-call(f32[256,4096]{1,0:T(8,128)S(1)} %copy-done), custom_call_target="tpu_custom_call" | custom-call | tf_op jit(solution)/shard_map/pallas_call | solution.py:295
  66.8 0.7 %copy.3 = f32[256,256]{1,0:T(8,128)} copy(f32[256,256]{1,0:T(8,128)S(1)} %shard_map.17) | data formatting | bytes 524288
Async XLA Ops:
  0.0 2.2 %copy-start = (f32[256,4096]{1,0:T(8,128)S(1)}, f32[256,4096]{1,0:T(8,128)}, u32[]{:S(2)}) copy-start(f32[256,4096]{1,0:T(8,128)} %x_ref.1) | copy-start | bytes 12582916
